TPU v7x, 32 devices: a whole 2x2x4 slice. The times are simulated.
32 devices in a mesh: lat: 4 (over y, x), lon: 8 (over z, core).
Axes of the slice: x: 2, y: 2, z: 4, core: 2. Of those that a mesh axis runs over, the one named last changes fastest.
Arguments:
- thickness: float32 [8, 128, 1024], P(None, 'lat', 'lon'), may hold values from 0.5 to 1.5
- winds: float32 [2, 8, 128, 1024], P(None, None, 'lat', 'lon'), may hold values from -2.5 to 2.5
- tracer_mass: float32 [8, 8, 128, 1024], P(None, None, 'lat', 'lon'), may hold values from -6 to 6
Outputs:
- thickness_out: float32 [8, 128, 1024], P(None, 'lat', 'lon')
- winds_out: float32 [2, 8, 128, 1024], P(None, None, 'lat', 'lon')
- tracer_out: float32 [8, 8, 128, 1024], P(None, None, 'lat', 'lon')
All inputs are finite; a program needn't handle non-finite values.
Results may differ from a plain program's by a relative error of at most 0.0003.
Values sent between devices are 32-bit elements; how exact they have to be, the bound alone decides.
A program may use at most 64 MiB of HBM per device.

v0:
```python
import math

import jax
import jax.numpy as jnp
from jax import lax
from jax.sharding import PartitionSpec as P

SUBSTEPS = 2


COUR = 0.25
GRAV = 1.0
FCOR = 1.0


def padded_2(cells, sides, width, closed):
    for axis, dim in sides:
        count = lax.axis_size(axis)
        ends = count if closed else count - 1
        head = lax.slice_in_dim(cells, 0, width, axis=dim)
        tail = lax.slice_in_dim(cells, cells.shape[dim] - width, cells.shape[dim], axis=dim)
        cells = jnp.concatenate(
            [
                lax.ppermute(tail, axis, [(i, (i + 1) % count) for i in range(ends)]),
                cells,
                lax.ppermute(head, axis, [((i + 1) % count, i) for i in range(ends)]),
            ],
            axis=dim,
        )
    return cells


def shifted(block, axis, distance):
    devices = range(lax.axis_size(axis))
    route = [((i - distance) % len(devices), i) for i in devices]
    return lax.ppermute(block, axis, route)


def geopot(thick):
    return GRAV * jnp.flip(jnp.cumsum(jnp.flip(thick, 0), 0), 0)


def upwind(face_speed, behind, centre, forward, beyond):
    return (
        face_speed
        * jnp.where(
            face_speed >= 0.0,
            5.0 * centre + 2.0 * forward - behind,
            5.0 * forward + 2.0 * centre - beyond,
        )
        / 6.0
    )


def advance(padded, potential, row_start, spacing):
    height = padded.shape[-2]
    columns = padded.shape[-1]
    row_index = (jnp.arange(height) + row_start).astype(jnp.float32)
    center_lat = (row_index[2 : height - 2] + 0.5) * spacing - 0.5 * math.pi
    face_lat = (row_index[1 : height - 2] + 1.0) * spacing - 0.5 * math.pi
    center_cos = jnp.cos(center_lat)[:, None]
    face_cos = jnp.abs(jnp.cos(face_lat))[:, None]
    coriolis = FCOR * jnp.sin(center_lat)[:, None] * jnp.where(center_cos >= 0.0, 1.0, -1.0)
    band_rows = padded[..., 2 : height - 2, :]
    zonal_wind = band_rows[1]
    face_speed = COUR * 0.5 * (zonal_wind[..., 1 : columns - 2] + zonal_wind[..., 2 : columns - 1])
    zonal_flux = upwind(
        face_speed,
        band_rows[..., 0 : columns - 3],
        band_rows[..., 1 : columns - 2],
        band_rows[..., 2 : columns - 1],
        band_rows[..., 3:columns],
    )
    zonal_div = zonal_flux[..., 1:] - zonal_flux[..., :-1]
    column_strip = padded[..., 2 : columns - 2]
    merid_wind = column_strip[2]
    merid_speed = (
        COUR
        * 0.5
        * (merid_wind[..., 1 : height - 2, :] + merid_wind[..., 2 : height - 1, :])
        * face_cos
    )
    merid_flux = upwind(
        merid_speed,
        column_strip[..., 0 : height - 3, :],
        column_strip[..., 1 : height - 2, :],
        column_strip[..., 2 : height - 1, :],
        column_strip[..., 3:height, :],
    )
    merid_div = (merid_flux[..., 1:, :] - merid_flux[..., :-1, :]) / jnp.abs(center_cos)
    center = padded[..., 2 : height - 2, 2 : columns - 2]
    advected = center - zonal_div - merid_div
    push_x = (
        COUR
        * 0.5
        * (
            potential[..., 2 : height - 2, 3 : columns - 1]
            - potential[..., 2 : height - 2, 1 : columns - 3]
        )
    )
    push_y = (
        COUR
        * 0.5
        * (
            potential[..., 3 : height - 1, 2 : columns - 2]
            - potential[..., 1 : height - 3, 2 : columns - 2]
        )
    )
    east_wind = advected[1] - push_x + COUR * coriolis * center[2]
    north_wind = advected[2] - push_y - COUR * coriolis * center[1]
    return jnp.concatenate([advected[0:1], east_wind[None], north_wind[None], advected[3:]], 0)


def extend(fields, margin, band_index):
    local_rows = fields.shape[2]
    last_band = lax.axis_size("lat") - 1
    lat_padded = padded_2(fields, (("lat", 2),), margin, False)
    sign_vector = jnp.where(jnp.arange(fields.shape[0]) == 2, -1.0, 1.0).astype(jnp.float32)[
        :, None, None, None
    ]
    south_rows = jnp.flip(fields[:, :, 0:margin], 2)
    north_rows = jnp.flip(fields[:, :, local_rows - margin :], 2)
    outgoing = jnp.where(band_index == 0, south_rows, north_rows) * sign_vector
    received = shifted(outgoing, "lon", lax.axis_size("lon") // 2)
    lat_padded = lat_padded.at[:, :, 0:margin].set(
        jnp.where(band_index == 0, received, lat_padded[:, :, 0:margin])
    )
    lat_padded = lat_padded.at[:, :, local_rows + margin :].set(
        jnp.where(band_index == last_band, received, lat_padded[:, :, local_rows + margin :])
    )
    return padded_2(lat_padded, (("lon", 3),), margin, True)


def shards(thickness, winds, tracer_mass):
    fields = jnp.concatenate([thickness[None], winds, tracer_mass], 0)
    local_rows = thickness.shape[1]
    spacing = math.pi / (local_rows * lax.axis_size("lat"))
    band_index = lax.axis_index("lat")
    for substep in range(SUBSTEPS):
        padded = extend(fields, 2, band_index)
        fields = advance(padded, geopot(padded[0]), band_index * local_rows - 2, spacing)
    return (fields[0], fields[1:3], fields[3:])


def solution(mesh):
    return jax.shard_map(
        shards,
        mesh=mesh,
        in_specs=(P(None, "lat", "lon"), P(None, None, "lat", "lon"), P(None, None, "lat", "lon")),
        out_specs=(P(None, "lat", "lon"), P(None, None, "lat", "lon"), P(None, None, "lat", "lon")),
        check_vma=False,
    )
```

profile of v0, /device:TPU:4, one launch (start us, length us, event | category | flops | bytes accessed | tf_op | source)
XLA Modules:
  0.0 88.9 jit_solution(14337706566130473052)
XLA Ops:
  0.6 1.4 %pad_maximum_fusion.6 = f32[11,8,32,128]{3,2,1,0:T(8,128)S(1)} fusion(f32[8,8,32,128]{3,2,1,0:T(8,128)} %param.13, f32[2,8,32,128]{3,2,1,0:T(8,128)} %param.12, f32[1,8,32,128]{3,2,1,0:T(8,128)} %bitcast.79), kind=kLoop, calls=%fused_computation.48 | loop fusion | flops 720896 | bytes 2883584 | tf_op jit(solution)/shard_map/concatenate | solution.py:135
  3.0 3.4 %collective-permute-start = (f32[11,8,2,128]{3,1,2,0:T(8,128)S(1)}, f32[11,8,2,128]{3,1,2,0:T(8,128)S(1)}, u32[]{:S(2)}, u32[]{:S(2)}) collective-permute-start(f32[11,8,2,128]{3,1,2,0:T(8,128)S(1)} %get-tuple-element.78), channel_id=1, source_target_pairs={{0,8},{8,16},{16,24},{1,9},{9,17},{17,25},{2,10},{10,18},{18,26},{... | collective-permute-start | bytes 270344 | tf_op jit(solution)/shard_map/ppermute | solution.py:24
  6.4 3.3 %collective-permute-start.1 = (f32[11,8,2,128]{3,1,2,0:T(8,128)S(1)}, f32[11,8,2,128]{3,1,2,0:T(8,128)S(1)}, u32[]{:S(2)}, u32[]{:S(2)}) collective-permute-start(f32[11,8,2,128]{3,1,2,0:T(8,128)S(1)} %get-tuple-element.79), channel_id=1, source_target_pairs={{8,0},{16,8},{24,16},{9,1},{17,9},{25,17},{10,2},{18,10},{26,18},{... | collective-permute-start | bytes 270344 | tf_op jit(solution)/shard_map/ppermute | solution.py:26
  9.9 2.6 %collective-permute-start.2 = (f32[11,8,2,128]{3,1,2,0:T(8,128)S(1)}, f32[11,8,2,128]{3,1,2,0:T(8,128)S(1)}, u32[]{:S(2)}, u32[]{:S(2)}) collective-permute-start(f32[11,8,2,128]{3,1,2,0:T(8,128)S(1)} %select_multiply_fusion.1), channel_id=1, source_target_pairs={{4,0},{5,1},{6,2},{7,3},{0,4},{1,5},{2,6},{3,7},{12,8},{13,9},{14,... | collective-permute-start | bytes 270344 | tf_op jit(solution)/shard_map/ppermute | solution.py:36
  13.0 3.6 %collective-permute-done.2 = f32[11,8,2,128]{3,1,2,0:T(8,128)S(1)} collective-permute-done((f32[11,8,2,128]{3,1,2,0:T(8,128)S(1)}, f32[11,8,2,128]{3,1,2,0:T(8,128)S(1)}, u32[]{:S(2)}, u32[]{:S(2)}) %collective-permute-start.2) | collective-permute-done | bytes 90144 | tf_op jit(solution)/shard_map/ppermute | solution.py:36
  16.7 1.7 %fusion.59 = (f32[11,8,36,2]{3,1,2,0:T(8,128)}, f32[11,8,36,2]{3,1,2,0:T(8,128)S(1)}) fusion(f32[11,8,36,128]{3,1,2,0:T(8,128)S(1)} %fusion.49), kind=kLoop, calls=%fused_computation.119 | loop fusion | bytes 101376 | tf_op jit(solution)/shard_map/slice | solution.py:21
  18.4 2.1 %copy.41 = f32[11,8,36,2]{2,1,3,0:T(8,128)S(1)} copy(f32[11,8,36,2]{3,1,2,0:T(8,128)} %get-tuple-element.74) | data formatting | bytes 50688 | tf_op jit(solution)/shard_map/slice | solution.py:21
  20.6 1.4 %copy.42 = f32[11,8,36,2]{2,1,3,0:T(8,128)} copy(f32[11,8,36,2]{3,1,2,0:T(8,128)S(1)} %get-tuple-element.75) | data formatting | bytes 50688 | tf_op jit(solution)/shard_map/slice | solution.py:20
  22.0 3.5 %collective-permute-start.4 = (f32[11,8,36,2]{2,1,3,0:T(8,128)}, f32[11,8,36,2]{2,1,3,0:T(8,128)}, u32[]{:S(2)}, u32[]{:S(2)}) collective-permute-start(f32[11,8,36,2]{2,1,3,0:T(8,128)} %copy.42), channel_id=1, source_target_pairs={{1,0},{2,1},{3,2},{4,3},{5,4},{6,5},{7,6},{0,7},{9,8},{10,9},{11,1... | collective-permute-start | bytes 76040 | tf_op jit(solution)/shard_map/ppermute | solution.py:26
  25.6 1.6 %fusion.19 = f32[11,8,33,128]{3,1,2,0:T(8,128)} fusion(f32[11,8,36,128]{3,1,2,0:T(8,128)S(1)} %fusion.49, f32[8,33,128]{2,0,1:T(8,128)S(1)} %get-tuple-element.67, pred[8,33,128]{2,0,1:T(8,128)(4,1)S(1)} %get-tuple-element.66), kind=kLoop, calls=%fused_computation.36 | loop fusion | flops 4088832 | bytes 7603200 | tf_op jit(solution)/shard_map/div | solution.py:45
  27.2 1.6 %copy.43 = f32[11,8,36,2]{3,1,2,0:T(8,128)S(1)} copy(f32[11,8,36,2]{2,1,3,0:T(8,128)} %collective-permute-done.3) | data formatting | bytes 50688 | tf_op jit(solution)/shard_map/ppermute | solution.py:24
  28.8 2.8 %copy.44 = f32[11,8,36,2]{3,1,2,0:T(8,128)} copy(f32[11,8,36,2]{2,1,3,0:T(8,128)} %collective-permute-done.4) | data formatting | bytes 50688 | tf_op jit(solution)/shard_map/ppermute | solution.py:26
  31.7 1.2 %fusion.27 = f32[8,36,132]{2,0,1:T(8,128)S(1)} fusion(f32[11,8,36,2]{3,1,2,0:T(8,128)} %copy.44, f32[11,8,36,128]{3,1,2,0:T(8,128)S(1)} %fusion.49, f32[11,8,36,2]{3,1,2,0:T(8,128)S(1)} %copy.43), kind=kLoop, calls=%fused_computation.53 | loop fusion | flops 76032 | bytes 1824768 | tf_op jit(solution)/shard_map/squeeze | solution.py:141
  33.6 3.2 %fusion.12 = f32[11,8,32,129]{3,1,2,0:T(8,128)S(1)} fusion(f32[11,8,36,2]{3,1,2,0:T(8,128)S(1)} %copy-done, f32[11,8,36,128]{3,1,2,0:T(8,128)S(1)} %fusion.49, f32[11,8,36,2]{3,1,2,0:T(8,128)S(1)} %copy.43, f32[8,32,129]{2,0,1:T(8,128)S(1)} %get-tuple-element.65, pred[8,32,129]{2,0,1:T(8,128)(4,1)S(1)} %get-tuple-element.64), kind=kLoop, calls=%fused_computation.23 | loop fusion | flops 5448960 | bytes 3290880 | tf_op jit(solution)/shard_map/div | solution.py:45
  39.2 1.2 %reduce_window_sum.17 = f32[8,36,132]{2,0,1:T(8,128)S(1)} reduce-window(f32[8,36,132]{2,0,1:T(8,128)} %rev.24, f32[]{:T(128)} %constant.142.clone.1), window={size=8x1x1 pad=7_0x0_0x0_0}, to_apply=%region_0.1 | reduce-window | flops 266112 | bytes 304132 | tf_op jit(solution)/shard_map/jit(cumsum)/reduce_window_sum | solution.py:40
  43.4 2.5 %collective-permute-start.5 = (f32[11,8,2,128]{3,1,2,0:T(8,128)S(1)}, f32[11,8,2,128]{3,1,2,0:T(8,128)S(1)}, u32[]{:S(2)}, u32[]{:S(2)}) collective-permute-start(f32[11,8,2,128]{3,1,2,0:T(8,128)S(1)} %get-tuple-element.76), channel_id=1, source_target_pairs={{0,8},{8,16},{16,24},{1,9},{9,17},{17,25},{2,10},{10,18},{18,26},{... | collective-permute-start | bytes 270344 | tf_op jit(solution)/shard_map/ppermute | solution.py:24
  45.9 4.2 %collective-permute-start.6 = (f32[11,8,2,128]{3,1,2,0:T(8,128)S(1)}, f32[11,8,2,128]{3,1,2,0:T(8,128)S(1)}, u32[]{:S(2)}, u32[]{:S(2)}) collective-permute-start(f32[11,8,2,128]{3,1,2,0:T(8,128)S(1)} %get-tuple-element.77), channel_id=1, source_target_pairs={{8,0},{16,8},{24,16},{9,1},{17,9},{25,17},{10,2},{18,10},{26,18},{... | collective-permute-start | bytes 270344 | tf_op jit(solution)/shard_map/ppermute | solution.py:26
  51.0 1.3 %collective-permute-done.6 = f32[11,8,2,128]{3,1,2,0:T(8,128)S(1)} collective-permute-done((f32[11,8,2,128]{3,1,2,0:T(8,128)S(1)}, f32[11,8,2,128]{3,1,2,0:T(8,128)S(1)}, u32[]{:S(2)}, u32[]{:S(2)}) %collective-permute-start.6) | collective-permute-done | bytes 90144 | tf_op jit(solution)/shard_map/ppermute | solution.py:26
  52.4 3.9 %collective-permute-done.7 = f32[11,8,2,128]{3,1,2,0:T(8,128)S(1)} collective-permute-done((f32[11,8,2,128]{3,1,2,0:T(8,128)S(1)}, f32[11,8,2,128]{3,1,2,0:T(8,128)S(1)}, u32[]{:S(2)}, u32[]{:S(2)}) %collective-permute-start.7) | collective-permute-done | bytes 90144 | tf_op jit(solution)/shard_map/ppermute | solution.py:36
  56.4 1.7 %fusion.58 = (f32[11,8,36,2]{3,1,2,0:T(8,128)}, f32[11,8,36,2]{3,1,2,0:T(8,128)S(1)}) fusion(f32[11,8,36,128]{3,1,2,0:T(8,128)S(1)} %fusion.48), kind=kLoop, calls=%fused_computation.118 | loop fusion | bytes 101376 | tf_op jit(solution)/shard_map/slice | solution.py:21
  58.2 2.1 %copy.47 = f32[11,8,36,2]{2,1,3,0:T(8,128)S(1)} copy(f32[11,8,36,2]{3,1,2,0:T(8,128)} %get-tuple-element.72) | data formatting | bytes 50688 | tf_op jit(solution)/shard_map/slice | solution.py:21
  60.4 1.4 %copy.48 = f32[11,8,36,2]{2,1,3,0:T(8,128)} copy(f32[11,8,36,2]{3,1,2,0:T(8,128)S(1)} %get-tuple-element.73) | data formatting | bytes 50688 | tf_op jit(solution)/shard_map/slice | solution.py:20
  61.7 3.5 %collective-permute-start.9 = (f32[11,8,36,2]{2,1,3,0:T(8,128)}, f32[11,8,36,2]{2,1,3,0:T(8,128)}, u32[]{:S(2)}, u32[]{:S(2)}) collective-permute-start(f32[11,8,36,2]{2,1,3,0:T(8,128)} %copy.48), channel_id=1, source_target_pairs={{1,0},{2,1},{3,2},{4,3},{5,4},{6,5},{7,6},{0,7},{9,8},{10,9},{11,1... | collective-permute-start | bytes 76040 | tf_op jit(solution)/shard_map/ppermute | solution.py:26
  65.4 1.6 %fusion.16 = f32[11,8,33,128]{3,1,2,0:T(8,128)} fusion(f32[11,8,36,128]{3,1,2,0:T(8,128)S(1)} %fusion.48, f32[8,33,128]{2,0,1:T(8,128)S(1)} %get-tuple-element.63, pred[8,33,128]{2,0,1:T(8,128)(4,1)S(1)} %get-tuple-element.62), kind=kLoop, calls=%fused_computation.31 | loop fusion | flops 4088832 | bytes 7603200 | tf_op jit(solution)/shard_map/div | solution.py:45
  66.9 1.6 %copy.49 = f32[11,8,36,2]{3,1,2,0:T(8,128)S(1)} copy(f32[11,8,36,2]{2,1,3,0:T(8,128)} %collective-permute-done.8) | data formatting | bytes 50688 | tf_op jit(solution)/shard_map/ppermute | solution.py:24
  68.6 2.8 %copy.50 = f32[11,8,36,2]{3,1,2,0:T(8,128)} copy(f32[11,8,36,2]{2,1,3,0:T(8,128)} %collective-permute-done.9) | data formatting | bytes 50688 | tf_op jit(solution)/shard_map/ppermute | solution.py:26
  71.4 1.2 %fusion.26 = f32[8,36,132]{2,0,1:T(8,128)S(1)} fusion(f32[11,8,36,2]{3,1,2,0:T(8,128)} %copy.50, f32[11,8,36,128]{3,1,2,0:T(8,128)S(1)} %fusion.48, f32[11,8,36,2]{3,1,2,0:T(8,128)S(1)} %copy.49), kind=kLoop, calls=%fused_computation.50 | loop fusion | flops 76032 | bytes 1824768 | tf_op jit(solution)/shard_map/squeeze | solution.py:141
  73.3 3.2 %fusion.7 = f32[11,8,32,129]{3,1,2,0:T(8,128)S(1)} fusion(f32[11,8,36,2]{3,1,2,0:T(8,128)S(1)} %copy-done.1, f32[11,8,36,128]{3,1,2,0:T(8,128)S(1)} %fusion.48, f32[11,8,36,2]{3,1,2,0:T(8,128)S(1)} %copy.49, f32[8,32,129]{2,0,1:T(8,128)S(1)} %get-tuple-element.61, pred[8,32,129]{2,0,1:T(8,128)(4,1)S(1)} %get-tuple-element.60), kind=kLoop, calls=%fused_computation.16 | loop fusion | flops 5448960 | bytes 3290880 | tf_op jit(solution)/shard_map/div | solution.py:45
  79.5 1.2 %reduce_window_sum.18 = f32[8,36,132]{2,0,1:T(8,128)S(1)} reduce-window(f32[8,36,132]{2,0,1:T(8,128)} %rev.27, f32[]{:T(128)} %constant.142.clone.1), window={size=8x1x1 pad=7_0x0_0x0_0}, to_apply=%region_1.2 | reduce-window | flops 266112 | bytes 304132 | tf_op jit(solution)/shard_map/jit(cumsum)/reduce_window_sum | solution.py:40
  83.5 1.6 %slice.455 = f32[8,32,128]{2,0,1:T(8,128)} reverse(f32[8,32,128]{2,0,1:T(8,128)} %get-tuple-element.81), dimensions={0} | reverse | bytes 262144 | tf_op jit(solution)/shard_map/slice | solution.py:106
  85.1 1.1 %fusion.38 = (f32[1,8,32,128]{3,1,2,0:T(8,128)S(1)}, f32[1,8,32,128]{3,1,2,0:T(8,128)S(1)}) fusion(f32[11,8,36,128]{3,1,2,0:T(8,128)S(1)} %fusion.48, f32[11,8,32,128]{3,1,2,0:T(8,128)S(1)} %fusion.21, f32[8,32,128]{2,0,1:T(8,128)S(1)} %slice.447, f32[8,32,128]{2,0,1:T(8,128)S(1)} %slice.449, f32[32]{0:T(128)S(1)} %get-tuple-element.88, ...), kind=kLoop, calls=%fused_computation.77 | loop fusion | flops 327680 | bytes 1310848 | tf_op jit(solution)/shard_map/broadcast_in_dim | solution.py:111
  86.4 1.2 %copy.56 = f32[8,8,32,128]{3,2,1,0:T(8,128)} copy(f32[8,8,32,128]{3,1,2,0:T(8,128)S(1)} %copy-done.5) | data formatting | bytes 2097152
  (69 shorter events, 16.9 us)
Async XLA Ops:
  3.0 9.8 %collective-permute-start = (f32[11,8,2,128]{3,1,2,0:T(8,128)S(1)}, f32[11,8,2,128]{3,1,2,0:T(8,128)S(1)}, u32[]{:S(2)}, u32[]{:S(2)}) collective-permute-start(f32[11,8,2,128]{3,1,2,0:T(8,128)S(1)} %get-tuple-element.78), channel_id=1, source_target_pairs={{0,8},{8,16},{16,24},{1,9},{9,17},{17,25},{2,10},{10,18},{18,26},{... | collective-permute-start | bytes 270344 | tf_op jit(solution)/shard_map/ppermute | solution.py:24
  6.4 6.4 %collective-permute-start.1 = (f32[11,8,2,128]{3,1,2,0:T(8,128)S(1)}, f32[11,8,2,128]{3,1,2,0:T(8,128)S(1)}, u32[]{:S(2)}, u32[]{:S(2)}) collective-permute-start(f32[11,8,2,128]{3,1,2,0:T(8,128)S(1)} %get-tuple-element.79), channel_id=1, source_target_pairs={{8,0},{16,8},{24,16},{9,1},{17,9},{25,17},{10,2},{18,10},{26,18},{... | collective-permute-start | bytes 270344 | tf_op jit(solution)/shard_map/ppermute | solution.py:26
  9.9 6.7 %collective-permute-start.2 = (f32[11,8,2,128]{3,1,2,0:T(8,128)S(1)}, f32[11,8,2,128]{3,1,2,0:T(8,128)S(1)}, u32[]{:S(2)}, u32[]{:S(2)}) collective-permute-start(f32[11,8,2,128]{3,1,2,0:T(8,128)S(1)} %select_multiply_fusion.1), channel_id=1, source_target_pairs={{4,0},{5,1},{6,2},{7,3},{0,4},{1,5},{2,6},{3,7},{12,8},{13,9},{14,... | collective-permute-start | bytes 270344 | tf_op jit(solution)/shard_map/ppermute | solution.py:36
  20.6 6.6 %collective-permute-start.3 = (f32[11,8,36,2]{2,1,3,0:T(8,128)S(1)}, f32[11,8,36,2]{2,1,3,0:T(8,128)}, u32[]{:S(2)}, u32[]{:S(2)}) collective-permute-start(f32[11,8,36,2]{2,1,3,0:T(8,128)S(1)} %copy.41), channel_id=1, source_target_pairs={{0,1},{1,2},{2,3},{3,4},{4,5},{5,6},{6,7},{7,0},{8,9},{9,10},{10,1... | collective-permute-start | bytes 76040 | tf_op jit(solution)/shard_map/ppermute | solution.py:24
  22.0 6.9 %collective-permute-start.4 = (f32[11,8,36,2]{2,1,3,0:T(8,128)}, f32[11,8,36,2]{2,1,3,0:T(8,128)}, u32[]{:S(2)}, u32[]{:S(2)}) collective-permute-start(f32[11,8,36,2]{2,1,3,0:T(8,128)} %copy.42), channel_id=1, source_target_pairs={{1,0},{2,1},{3,2},{4,3},{5,4},{6,5},{7,6},{0,7},{9,8},{10,9},{11,1... | collective-permute-start | bytes 76040 | tf_op jit(solution)/shard_map/ppermute | solution.py:26
  31.7 1.5 %copy-start = (f32[11,8,36,2]{3,1,2,0:T(8,128)S(1)}, f32[11,8,36,2]{3,1,2,0:T(8,128)}, u32[]{:S(2)}) copy-start(f32[11,8,36,2]{3,1,2,0:T(8,128)} %copy.44) | copy-start | bytes 76036
  33.6 3.2 %copy-start.3 = (f32[11,8,33,128]{3,1,2,0:T(8,128)S(1)}, f32[11,8,33,128]{3,1,2,0:T(8,128)}, u32[]{:S(2)}) copy-start(f32[11,8,33,128]{3,1,2,0:T(8,128)} %fusion.19) | copy-start | bytes 4460548
  37.3 1.1 %copy-start.4 = (f32[11,8,32,128]{3,1,2,0:T(8,128)}, f32[11,8,32,128]{3,1,2,0:T(8,128)S(1)}, u32[]{:S(2)}) copy-start(f32[11,8,32,128]{3,1,2,0:T(8,128)S(1)} %fusion.24) | copy-start | bytes 4325380
  43.4 7.7 %collective-permute-start.5 = (f32[11,8,2,128]{3,1,2,0:T(8,128)S(1)}, f32[11,8,2,128]{3,1,2,0:T(8,128)S(1)}, u32[]{:S(2)}, u32[]{:S(2)}) collective-permute-start(f32[11,8,2,128]{3,1,2,0:T(8,128)S(1)} %get-tuple-element.76), channel_id=1, source_target_pairs={{0,8},{8,16},{16,24},{1,9},{9,17},{17,25},{2,10},{10,18},{18,26},{... | collective-permute-start | bytes 270344 | tf_op jit(solution)/shard_map/ppermute | solution.py:24
  45.9 6.4 %collective-permute-start.6 = (f32[11,8,2,128]{3,1,2,0:T(8,128)S(1)}, f32[11,8,2,128]{3,1,2,0:T(8,128)S(1)}, u32[]{:S(2)}, u32[]{:S(2)}) collective-permute-start(f32[11,8,2,128]{3,1,2,0:T(8,128)S(1)} %get-tuple-element.77), channel_id=1, source_target_pairs={{8,0},{16,8},{24,16},{9,1},{17,9},{25,17},{10,2},{18,10},{26,18},{... | collective-permute-start | bytes 270344 | tf_op jit(solution)/shard_map/ppermute | solution.py:26
  50.2 6.1 %collective-permute-start.7 = (f32[11,8,2,128]{3,1,2,0:T(8,128)S(1)}, f32[11,8,2,128]{3,1,2,0:T(8,128)S(1)}, u32[]{:S(2)}, u32[]{:S(2)}) collective-permute-start(f32[11,8,2,128]{3,1,2,0:T(8,128)S(1)} %select_multiply_fusion), channel_id=1, source_target_pairs={{4,0},{5,1},{6,2},{7,3},{0,4},{1,5},{2,6},{3,7},{12,8},{13,9},{14,... | collective-permute-start | bytes 270344 | tf_op jit(solution)/shard_map/ppermute | solution.py:36
  60.3 6.6 %collective-permute-start.8 = (f32[11,8,36,2]{2,1,3,0:T(8,128)S(1)}, f32[11,8,36,2]{2,1,3,0:T(8,128)}, u32[]{:S(2)}, u32[]{:S(2)}) collective-permute-start(f32[11,8,36,2]{2,1,3,0:T(8,128)S(1)} %copy.47), channel_id=1, source_target_pairs={{0,1},{1,2},{2,3},{3,4},{4,5},{5,6},{6,7},{7,0},{8,9},{9,10},{10,1... | collective-permute-start | bytes 76040 | tf_op jit(solution)/shard_map/ppermute | solution.py:24
  61.7 6.9 %collective-permute-start.9 = (f32[11,8,36,2]{2,1,3,0:T(8,128)}, f32[11,8,36,2]{2,1,3,0:T(8,128)}, u32[]{:S(2)}, u32[]{:S(2)}) collective-permute-start(f32[11,8,36,2]{2,1,3,0:T(8,128)} %copy.48), channel_id=1, source_target_pairs={{1,0},{2,1},{3,2},{4,3},{5,4},{6,5},{7,6},{0,7},{9,8},{10,9},{11,1... | collective-permute-start | bytes 76040 | tf_op jit(solution)/shard_map/ppermute | solution.py:26
  71.4 1.5 %copy-start.1 = (f32[11,8,36,2]{3,1,2,0:T(8,128)S(1)}, f32[11,8,36,2]{3,1,2,0:T(8,128)}, u32[]{:S(2)}) copy-start(f32[11,8,36,2]{3,1,2,0:T(8,128)} %copy.50) | copy-start | bytes 76036
  73.3 3.2 %copy-start.2 = (f32[11,8,33,128]{3,1,2,0:T(8,128)S(1)}, f32[11,8,33,128]{3,1,2,0:T(8,128)}, u32[]{:S(2)}) copy-start(f32[11,8,33,128]{3,1,2,0:T(8,128)} %fusion.16) | copy-start | bytes 4460548
  85.1 1.3 %copy-start.5 = (f32[8,8,32,128]{3,1,2,0:T(8,128)S(1)}, f32[8,8,32,128]{3,1,2,0:T(8,128)}, u32[]{:S(2)}) copy-start(f32[8,8,32,128]{3,1,2,0:T(8,128)} %slice.521) | copy-start | bytes 3145732
  86.2 1.3 %copy-start.6 = (f32[8,32,128]{2,0,1:T(8,128)S(1)}, f32[8,32,128]{2,0,1:T(8,128)}, u32[]{:S(2)}) copy-start(f32[8,32,128]{2,0,1:T(8,128)} %slice_bitcast_fusion.6) | copy-start | bytes 393220
where the time goes:
time: 89.6 us; the launch traced here: 88.9 us
  local copies, waits for them, and re-layouts  33.5 us (37%)
  starting transfers between devices  23.3 us (26%)
  other arithmetic  21.4 us (24%)
  waiting for transfers between devices  9.67 us (11%)
  between operations  1.04 us (1%)
    ppermute x4, starting transfers between devices, padded_2(): lax.ppermute(head, axis, [((i + 1) % count, i) for i in range(ends)])  14.6 us
    div x4, other arithmetic, upwind(): face_speed * jnp.where(face_speed >= 0.0, 5.0 * centre + 2.0 * forward -...  9.5 us
    slice x5, local copies, waits for them, and re-layouts, padded_2(): lax.slice_in_dim(cells, cells.shape[dim] - width, cells.shape[dim], axis=...  7.78 us
    ppermute x2, waiting for transfers between devices, shifted(): return lax.ppermute(block, axis, route)  7.58 us
    ppermute x4, starting transfers between devices, padded_2(): lax.ppermute(tail, axis, [(i, (i + 1) % count) for i in range(ends)])  5.99 us
    ppermute x2, local copies, waits for them, and re-layouts, padded_2(): lax.ppermute(head, axis, [((i + 1) % count, i) for i in range(ends)])  5.65 us
    unnamed x16, local copies, waits for them, and re-layouts  3.56 us
    ppermute x2, local copies, waits for them, and re-layouts, padded_2(): lax.ppermute(tail, axis, [(i, (i + 1) % count) for i in range(ends)])  3.27 us
  transfers between devices with their start and end apart: 10, of which 5 were waited for; matrix products, arithmetic and copies ran while one was open for 11% of the time, Pallas kernels for 0%

commit v1 on v0

v1 whole, which is shorter than its diff:
```python
import functools
import math

import jax
import jax.numpy as jnp
from jax import lax
from jax.experimental import pallas as pl
from jax.experimental.pallas import tpu as pltpu
from jax.sharding import PartitionSpec as P

SUBSTEPS = 2
COUR = 0.25
GRAV = 1.0
FCOR = 1.0
TG = 2
MESH = pl.DeviceIdType.MESH


def kernel(nlat, nlon, h_hbm, w_hbm, t_hbm, ho, wo, to, hin, win, tin, S, Gs, As, Bs, DXs, DYs, invc, corr, facec,
           rs, rr, cs, cr, hv, wv, tv, in_sem, out_sem, send_sem, recv_sem):
    lev, rows, cols = hin.shape
    ntr = tin.shape[0]
    ngroups = 1 + ntr // TG
    G8 = rows // 8
    stride = rows + 8
    width = 4
    band = lax.axis_index("lat")
    lon = lax.axis_index("lon")
    first = (nlat - band) // nlat
    last = (band + 1) // nlat
    half = nlon // 2
    south = (band - 1 + first, lax.rem(lon + first * half, nlon))
    north = (band + 1 - last, lax.rem(lon + last * half, nlon))
    east = (band, lax.rem(lon + 1, nlon))
    west = (band, lax.rem(lon + nlon - 1, nlon))
    sgn_s = (1 - 2 * first).astype(jnp.float32)
    sgn_n = (1 - 2 * last).astype(jnp.float32)

    barrier = pltpu.get_barrier_semaphore()
    for peer in (south, north, east, west):
        pl.semaphore_signal(barrier, inc=1, device_id=peer, device_id_type=MESH)
    loads = [
        pltpu.make_async_copy(h_hbm, hin, in_sem.at[0]),
        pltpu.make_async_copy(w_hbm, win, in_sem.at[1]),
        pltpu.make_async_copy(t_hbm, tin, in_sem.at[2]),
    ]
    for load in loads:
        load.start()

    spacing = math.pi / (rows * nlat)
    row = lax.broadcasted_iota(jnp.int32, (rows, cols), 0)
    rowf = (row + band * rows).astype(jnp.float32)
    centre_lat = (rowf + 0.5) * spacing - 0.5 * math.pi
    invc[...] = 1.0 / jnp.cos(centre_lat)
    corr[...] = (COUR * FCOR) * jnp.sin(centre_lat)
    face_lat = (rowf + 1.0) * spacing - 0.5 * math.pi
    facec[...] = jnp.abs(jnp.cos(face_lat)) * (COUR * 0.5 / 6.0)
    low_row = (lax.broadcasted_iota(jnp.int32, (8, cols), 0) * 0 + band * rows).astype(jnp.float32)
    fcL = jnp.abs(jnp.cos(low_row * spacing - 0.5 * math.pi)) * (COUR * 0.5 / 6.0)

    lane = lax.broadcasted_iota(jnp.int32, (rows, cols), 1)
    lane8 = lax.broadcasted_iota(jnp.int32, (8, cols), 1)
    slot8 = lane8 // width
    low8 = lax.rem(lane8, width) < 2
    first_lane = lane < 1
    two_lanes = lane < 2
    last_lane = lane >= cols - 1

    def face(speed, behind, centre, forward, beyond):
        return speed * jnp.where(
            speed >= 0.0, 5.0 * centre + 2.0 * forward - behind, 5.0 * forward + 2.0 * centre - beyond
        )

    def pack(acc, x, l):
        for rg in range(G8):
            k = l * G8 + rg
            acc = jnp.where(slot8 == k, pltpu.roll(x[8 * rg : 8 * rg + 8], width * k + 2, 1), acc)
        return acc

    def unpack(packed, l):
        return jnp.concatenate(
            [pltpu.roll(packed, cols - 2 - width * (l * G8 + rg), 1) for rg in range(G8)], 0
        )

    def pack_rows(s, f):
        for r in range(2):
            lo = S[s, f, pl.ds(8 + r + first * (1 - 2 * r), lev, stride=stride), :]
            hi = S[s, f, pl.ds(8 + rows - 2 + r + last * (1 - 2 * r), lev, stride=stride), :]
            if isinstance(f, int) and f == 2:
                lo, hi = lo * sgn_s, hi * sgn_n
            rs[s, 0, f, r] = lo
            rs[s, 1, f, r] = hi

    def copies(s, f0, nf, g):
        fs = pl.ds(f0, nf)

        def one(src, dst, n, m, peer):
            return pltpu.make_async_remote_copy(
                src_ref=src, dst_ref=dst, send_sem=send_sem.at[s, n, g], recv_sem=recv_sem.at[s, m, g],
                device_id=peer, device_id_type=MESH,
            )

        return [
            one(rs.at[s, 0, fs], rr.at[s, 1 - first, fs], 0, 1 - first, south),
            one(rs.at[s, 1, fs], rr.at[s, last, fs], 1, last, north),
            one(cs.at[s, fs], cr.at[s, 0, fs], 2, 2, east),
            one(cs.at[s, fs], cr.at[s, 1, fs], 3, 3, west),
        ]

    def send(s, f0, nf, g):
        for c in copies(s, f0, nf, g):
            c.start()

    def await_halo(s, f0, nf, g):
        fs = pl.ds(f0, nf)
        for m in range(4):
            dst = rr.at[s, m, fs] if m < 2 else cr.at[s, m - 2, fs]
            src = rs.at[s, m, fs] if m < 2 else cs.at[s, fs]
            pltpu.make_async_remote_copy(
                src_ref=src, dst_ref=dst, send_sem=send_sem.at[s, m, g], recv_sem=recv_sem.at[s, m, g],
                device_id=east, device_id_type=MESH,
            ).wait_recv()

    def stage(f, read):
        def level(l, acc):
            x = read(l)
            S[0, f, pl.ds(stride * l + 8, rows), :] = x
            return pack(acc, x, l)

        cs[0, f] = lax.fori_loop(0, lev, level, jnp.zeros((8, cols), jnp.float32), unroll=True)
        pack_rows(0, f)

    loads[0].wait()
    loads[1].wait()
    stage(0, lambda l: hin[l])
    stage(1, lambda l: win[0, l])
    stage(2, lambda l: win[1, l])
    pl.semaphore_wait(barrier, 4)
    send(0, 0, 3, 0)
    loads[2].wait()

    def stage_group(g, c):
        for t in range(TG):
            i = g * TG + t
            stage(3 + i, lambda l: tin[i, l])
        send(0, 3 + g * TG, TG, g + 1)
        return c

    lax.fori_loop(0, ngroups - 1, stage_group, 0)

    for s in range(SUBSTEPS):
        final = s == SUBSTEPS - 1

        def place_rows(f):
            S[s, f, pl.ds(7, lev, stride=stride), :] = rr[s, 0, f, 1]
            S[s, f, pl.ds(8 + rows, lev, stride=stride), :] = rr[s, 1, f, 0]
            S[s, f, pl.ds(9 + rows, lev, stride=stride), :] = rr[s, 1, f, 1]

        def side(f):
            return jnp.where(low8, cr[s, 0, f], cr[s, 1, f]), jnp.where(low8, cr[s, 0, f], cs[s, f])

        def core(f, d=0):
            return lambda l: S[s, f, pl.ds(stride * l + 8 + d, rows), :]

        await_halo(s, 0, 3, 0)
        for f in range(3):
            place_rows(f)
        Cu, Lu = side(1)
        aL = (COUR * 0.5 / 6.0) * (Lu + pltpu.roll(Lu, cols - 1, 1))
        bL = fcL * (rr[s, 0, 2, 1] + S[s, 2, pl.ds(8, lev, stride=stride), :])

        def speeds(l, c):
            u = core(1)(l)
            up = pltpu.roll(jnp.where(first_lane, unpack(Cu, l), u), cols - 1, 1)
            As[l] = (COUR * 0.5 / 6.0) * (u + up)
            Bs[l] = facec[...] * (core(2)(l) + core(2, 1)(l))
            return c

        lax.fori_loop(0, lev, speeds, 0, unroll=True)

        def field(f, write, kind):
            C, L = side(f)
            Lp = pltpu.roll(L, cols - 1, 1)
            FL = face(aL, pltpu.roll(L, 1, 1), L, Lp, pltpu.roll(L, cols - 2, 1))
            x0 = S[s, f, pl.ds(8, lev, stride=stride), :]
            x1 = S[s, f, pl.ds(9, lev, stride=stride), :]
            Gs[pl.ds(7, lev, stride=stride), :] = face(bL, rr[s, 0, f, 0], rr[s, 0, f, 1], x0, x1)

            def level(i, carry):
                l = lev - 1 - i
                acc, dx, dy = carry
                x = core(f)(l)
                H = unpack(C, l)
                xp = pltpu.roll(jnp.where(first_lane, H, x), cols - 1, 1)
                xpp = pltpu.roll(jnp.where(two_lanes, H, x), cols - 2, 1)
                xm = pltpu.roll(jnp.where(last_lane, H, x), 1, 1)
                F = face(As[l], xm, x, xp, xpp)
                Fl = pltpu.roll(jnp.where(last_lane, unpack(FL, l), F), 1, 1)
                ym, yp, ypp = core(f, -1)(l), core(f, 1)(l), core(f, 2)(l)
                G = face(Bs[l], ym, x, yp, ypp)
                Gs[pl.ds(stride * l + 8, rows), :] = G
                Gl = Gs[pl.ds(stride * l + 7, rows), :]
                new = x - (F - Fl) - (G - Gl) * invc[...]
                if kind == 0:
                    dx = dx + (xp - xm)
                    dy = dy + (yp - ym)
                    DXs[l] = dx
                    DYs[l] = dy
                elif kind == 1:
                    new = new - (COUR * 0.5 * GRAV) * DXs[l] + corr[...] * core(2)(l)
                elif kind == 2:
                    new = new - (COUR * 0.5 * GRAV) * DYs[l] - corr[...] * core(1)(l)
                if final:
                    write(l, new)
                else:
                    S[s + 1, f, pl.ds(stride * l + 8, rows), :] = new
                    acc = pack(acc, new, l)
                return acc, dx, dy

            if kind == 0:
                zero = jnp.zeros((rows, cols), jnp.float32)
            else:
                zero = 0
            acc0 = 0 if final else jnp.zeros((8, cols), jnp.float32)
            acc = lax.fori_loop(0, lev, level, (acc0, zero, zero), unroll=True)[0]
            if not final:
                cs[s + 1, f] = acc
                pack_rows(s + 1, f)

        def write_h(l, x):
            hv[l] = x

        def write_u(l, x):
            wv[0, l] = x

        def write_v(l, x):
            wv[1, l] = x

        field(0, write_h, 0)
        field(1, write_u, 1)
        field(2, write_v, 2)
        if final:
            pltpu.make_async_copy(hv, ho, out_sem.at[0]).start()
            pltpu.make_async_copy(wv, wo, out_sem.at[1]).start()
        else:
            send(s + 1, 0, 3, 0)

        def tracers(g, c):
            await_halo(s, 3 + g * TG, TG, g + 1)
            for t in range(TG):
                i = g * TG + t

                def write_t(l, x):
                    tv[i, l] = x

                place_rows(3 + i)
                field(3 + i, write_t, 3)
            if final:
                ts = pl.ds(g * TG, TG)
                pltpu.make_async_copy(tv.at[ts], to.at[ts], out_sem.at[g + 2]).start()
            else:
                send(s + 1, 3 + g * TG, TG, g + 1)
            return c

        lax.fori_loop(0, ngroups - 1, tracers, 0)

    for s in range(SUBSTEPS):
        for c in copies(s, 0, 3, 0):
            c.wait_send()

        def drain(g, c):
            for d in copies(s, 3 + g * TG, TG, g + 1):
                d.wait_send()
            return c

        lax.fori_loop(0, ngroups - 1, drain, 0)
    pltpu.make_async_copy(hv, ho, out_sem.at[0]).wait()
    pltpu.make_async_copy(wv, wo, out_sem.at[1]).wait()

    def flush(g, c):
        ts = pl.ds(g * TG, TG)
        pltpu.make_async_copy(tv.at[ts], to.at[ts], out_sem.at[g + 2]).wait()
        return c

    lax.fori_loop(0, ngroups - 1, flush, 0)


def shards(nlat, nlon, thickness, winds, tracer_mass):
    lev, rows, cols = thickness.shape
    ntr = tracer_mass.shape[0]
    nf = 3 + ntr
    groups = 1 + ntr // TG
    f32 = jnp.float32
    flat = lev * (rows + 8) + 8
    vm = pltpu.VMEM
    return pl.pallas_call(
        functools.partial(kernel, nlat, nlon),
        out_shape=[jax.ShapeDtypeStruct(a.shape, f32) for a in (thickness, winds, tracer_mass)],
        in_specs=[pl.BlockSpec(memory_space=pl.ANY)] * 3,
        out_specs=[pl.BlockSpec(memory_space=pl.ANY)] * 3,
        scratch_shapes=[
            vm(thickness.shape, f32),
            vm(winds.shape, f32),
            vm(tracer_mass.shape, f32),
            vm((SUBSTEPS, nf, flat, cols), f32),
            vm((flat, cols), f32),
            vm((lev, rows, cols), f32),
            vm((lev, rows, cols), f32),
            vm((lev, rows, cols), f32),
            vm((lev, rows, cols), f32),
            vm((rows, cols), f32),
            vm((rows, cols), f32),
            vm((rows, cols), f32),
            vm((SUBSTEPS, 2, nf, 2, lev, cols), f32),
            vm((SUBSTEPS, 2, nf, 2, lev, cols), f32),
            vm((SUBSTEPS, nf, 8, cols), f32),
            vm((SUBSTEPS, 2, nf, 8, cols), f32),
            vm(thickness.shape, f32),
            vm(winds.shape, f32),
            vm(tracer_mass.shape, f32),
            pltpu.SemaphoreType.DMA((3,)),
            pltpu.SemaphoreType.DMA((groups + 1,)),
            pltpu.SemaphoreType.DMA((SUBSTEPS, 4, groups)),
            pltpu.SemaphoreType.DMA((SUBSTEPS, 4, groups)),
        ],
        compiler_params=pltpu.CompilerParams(
            collective_id=0, has_side_effects=True, vmem_limit_bytes=32 * 1024 * 1024
        ),
        cost_estimate=pl.CostEstimate(flops=30_000_000, bytes_accessed=3_000_000, transcendentals=0),
    )(thickness, winds, tracer_mass)


def solution(mesh):
    specs = (P(None, "lat", "lon"), P(None, None, "lat", "lon"), P(None, None, "lat", "lon"))
    return jax.shard_map(
        functools.partial(shards, mesh.shape["lat"], mesh.shape["lon"]),
        mesh=mesh,
        in_specs=specs,
        out_specs=specs,
        check_vma=False,
    )
```

time: 89.6 us -> 37.8 us (0.42)
  the two profiles are of different devices: /device:TPU:4 before, /device:TPU:0 now
where the time goes in v1:
time: 37.8 us; the launch traced here: 37.5 us
  Pallas kernels  31.5 us (83%)
  local copies, waits for them, and re-layouts  5.4 us (14%)
  between operations  0.65 us (2%)
    pallas_call x1, Pallas kernels, shards(): pl.pallas_call(functools.partial(kernel, nlat, nlon), out_shape=[jax.Shap...  31.5 us
    unnamed x9, local copies, waits for them, and re-layouts  5.4 us

profile of v1, /device:TPU:0, one launch (start us, length us, event | category | flops | bytes accessed | tf_op | source)
XLA Modules:
  0.0 37.5 jit_solution(15934347465508724443)
XLA Ops:
  0.6 0.0 copy-start
  0.6 1.2 %copy-done = f32[8,8,32,128]{3,2,1,0:T(8,128)S(1)} copy-done((f32[8,8,32,128]{3,2,1,0:T(8,128)S(1)}, f32[8,8,32,128]{3,2,1,0:T(8,128)}, u32[]{:S(2)}) %copy-start) | copy-done | bytes 1048600
  1.9 0.0 copy-start.1
  1.9 0.9 %copy-done.1 = f32[2,8,32,128]{3,2,1,0:T(8,128)S(1)} copy-done((f32[2,8,32,128]{3,2,1,0:T(8,128)S(1)}, f32[2,8,32,128]{3,2,1,0:T(8,128)}, u32[]{:S(2)}) %copy-start.1) | copy-done | bytes 262168
  2.8 0.0 copy-start.2
  2.8 0.9 %copy-done.2 = f32[8,32,128]{2,1,0:T(8,128)S(1)} copy-done((f32[8,32,128]{2,1,0:T(8,128)S(1)}, f32[8,32,128]{2,1,0:T(8,128)}, u32[]{:S(2)}) %copy-start.2) | copy-done | bytes 131096
  3.7 31.5 %shard_map.58 = (f32[8,32,128]{2,1,0:T(8,128)S(1)}, f32[2,8,32,128]{3,2,1,0:T(8,128)S(1)}, f32[8,8,32,128]{3,2,1,0:T(8,128)S(1)}) custom-call(f32[8,32,128]{2,1,0:T(8,128)S(1)} %copy-done.2, f32[2,8,32,128]{3,2,1,0:T(8,128)S(1)} %copy-done.1, f32[8,8,32,128]{3,2,1,0:T(8,128)S(1)} %copy-done), custom_call_target="tpu_custom_call" | custom-call | flops 30000000 | bytes 3000000 | tf_op jit(solution)/shard_map/pallas_call | solution.py:296
  35.2 0.7 %copy.9 = f32[8,32,128]{2,1,0:T(8,128)} copy(f32[8,32,128]{2,1,0:T(8,128)S(1)} %get-tuple-element.6) | data formatting | bytes 262144
  35.9 0.7 %copy.10 = f32[2,8,32,128]{3,2,1,0:T(8,128)} copy(f32[2,8,32,128]{3,2,1,0:T(8,128)S(1)} %get-tuple-element.7) | data formatting | bytes 524288
  36.6 1.0 %copy.11 = f32[8,8,32,128]{3,2,1,0:T(8,128)} copy(f32[8,8,32,128]{3,2,1,0:T(8,128)S(1)} %get-tuple-element.8) | data formatting | bytes 2097152
Async XLA Ops:
  0.6 1.2 %copy-start = (f32[8,8,32,128]{3,2,1,0:T(8,128)S(1)}, f32[8,8,32,128]{3,2,1,0:T(8,128)}, u32[]{:S(2)}) copy-start(f32[8,8,32,128]{3,2,1,0:T(8,128)} %t_hbm.1) | copy-start | bytes 3145732
  1.9 0.9 %copy-start.1 = (f32[2,8,32,128]{3,2,1,0:T(8,128)S(1)}, f32[2,8,32,128]{3,2,1,0:T(8,128)}, u32[]{:S(2)}) copy-start(f32[2,8,32,128]{3,2,1,0:T(8,128)} %w_hbm.1) | copy-start | bytes 786436
  2.8 0.9 %copy-start.2 = (f32[8,32,128]{2,1,0:T(8,128)S(1)}, f32[8,32,128]{2,1,0:T(8,128)}, u32[]{:S(2)}) copy-start(f32[8,32,128]{2,1,0:T(8,128)} %h_hbm.1) | copy-start | bytes 393220

commit v2 on v1

v2 whole, which is shorter than its diff:
```python
import functools
import math

import jax
import jax.numpy as jnp
from jax import lax
from jax.experimental import pallas as pl
from jax.experimental.pallas import tpu as pltpu
from jax.sharding import PartitionSpec as P

SUBSTEPS = 2
COUR = 0.25
GRAV = 1.0
FCOR = 1.0
TG = 2
MESH = pl.DeviceIdType.MESH


def kernel(nlat, nlon, h_hbm, w_hbm, t_hbm, ho, wo, to, xin, S, Gs, As, Bs, frc, invc, corr, facec,
           rs, rr, cs, cr, out, in_sem, out_sem, send_sem, recv_sem):
    nf, lev, rows, cols = xin.shape
    ngroups = 1 + (nf - 3) // TG
    G8 = rows // 8
    stride = rows + 8
    width = 4
    band = lax.axis_index("lat")
    lon = lax.axis_index("lon")
    first = (nlat - band) // nlat
    last = (band + 1) // nlat
    half = nlon // 2
    south = (band - 1 + first, lax.rem(lon + first * half, nlon))
    north = (band + 1 - last, lax.rem(lon + last * half, nlon))
    east = (band, lax.rem(lon + 1, nlon))
    west = (band, lax.rem(lon + nlon - 1, nlon))

    barrier = pltpu.get_barrier_semaphore()
    for peer in (south, north, east, west):
        pl.semaphore_signal(barrier, inc=1, device_id=peer, device_id_type=MESH)
    loads = [
        pltpu.make_async_copy(h_hbm, xin.at[0], in_sem.at[0]),
        pltpu.make_async_copy(w_hbm, xin.at[pl.ds(1, 2)], in_sem.at[1]),
        pltpu.make_async_copy(t_hbm, xin.at[pl.ds(3, nf - 3)], in_sem.at[2]),
    ]
    for load in loads:
        load.start()

    spacing = math.pi / (rows * nlat)
    row = lax.broadcasted_iota(jnp.int32, (rows, cols), 0)
    rowf = (row + band * rows).astype(jnp.float32)
    centre_lat = (rowf + 0.5) * spacing - 0.5 * math.pi
    invc[...] = 1.0 / jnp.cos(centre_lat)
    corr[...] = (COUR * FCOR) * jnp.sin(centre_lat)
    face_lat = (rowf + 1.0) * spacing - 0.5 * math.pi
    facec[...] = jnp.abs(jnp.cos(face_lat)) * (COUR * 0.5 / 6.0)
    low_row = (lax.broadcasted_iota(jnp.int32, (8, cols), 0) * 0 + band * rows).astype(jnp.float32)
    fcL = jnp.abs(jnp.cos(low_row * spacing - 0.5 * math.pi)) * (COUR * 0.5 / 6.0)
    frc[0] = jnp.zeros((lev, rows, cols), jnp.float32)

    lane = lax.broadcasted_iota(jnp.int32, (rows, cols), 1)
    lane8 = lax.broadcasted_iota(jnp.int32, (8, cols), 1)
    slot8 = lane8 // width
    low8 = lax.rem(lane8, width) < 2
    first_lane = lane < 1
    two_lanes = lane < 2
    last_lane = lane >= cols - 1

    def face(speed, behind, centre, forward, beyond):
        return speed * jnp.where(
            speed >= 0.0, 5.0 * centre + 2.0 * forward - behind, 5.0 * forward + 2.0 * centre - beyond
        )

    def pack(acc, x, l):
        for rg in range(G8):
            k = l * G8 + rg
            acc = jnp.where(slot8 == k, pltpu.roll(x[8 * rg : 8 * rg + 8], width * k + 2, 1), acc)
        return acc

    def unpack(packed, l):
        return jnp.concatenate(
            [pltpu.roll(packed, cols - 2 - width * (l * G8 + rg), 1) for rg in range(G8)], 0
        )

    def wind(f):
        return f * ((nf + 2 - f) // nf)

    def pack_rows(s, f):
        is_v = wind(f) // 2
        for r in range(2):
            lo = S[s, f, pl.ds(8 + r + first * (1 - 2 * r), lev, stride=stride), :]
            hi = S[s, f, pl.ds(8 + rows - 2 + r + last * (1 - 2 * r), lev, stride=stride), :]
            rs[s, 0, f, r] = lo * (1 - 2 * first * is_v).astype(jnp.float32)
            rs[s, 1, f, r] = hi * (1 - 2 * last * is_v).astype(jnp.float32)

    def copies(s, f0, n, g):
        fs = pl.ds(f0, n)

        def one(src, dst, k, m, peer):
            return pltpu.make_async_remote_copy(
                src_ref=src, dst_ref=dst, send_sem=send_sem.at[s, k, g], recv_sem=recv_sem.at[s, m, g],
                device_id=peer, device_id_type=MESH,
            )

        return [
            one(rs.at[s, 0, fs], rr.at[s, 1 - first, fs], 0, 1 - first, south),
            one(rs.at[s, 1, fs], rr.at[s, last, fs], 1, last, north),
            one(cs.at[s, fs], cr.at[s, 0, fs], 2, 2, east),
            one(cs.at[s, fs], cr.at[s, 1, fs], 3, 3, west),
        ]

    def send(s, f0, n, g):
        for c in copies(s, f0, n, g):
            c.start()

    def await_halo(s, f0, n, g):
        fs = pl.ds(f0, n)
        for m in range(4):
            dst = rr.at[s, m, fs] if m < 2 else cr.at[s, m - 2, fs]
            src = rs.at[s, m, fs] if m < 2 else cs.at[s, fs]
            pltpu.make_async_remote_copy(
                src_ref=src, dst_ref=dst, send_sem=send_sem.at[s, m, g], recv_sem=recv_sem.at[s, m, g],
                device_id=east, device_id_type=MESH,
            ).wait_recv()

    def stage(f, c):
        def level(l, acc):
            x = xin[f, l]
            S[0, f, pl.ds(stride * l + 8, rows), :] = x
            return pack(acc, x, l)

        cs[0, f] = lax.fori_loop(0, lev, level, jnp.zeros((8, cols), jnp.float32), unroll=True)
        pack_rows(0, f)
        return c

    loads[0].wait()
    loads[1].wait()
    lax.fori_loop(0, 3, stage, 0)
    pl.semaphore_wait(barrier, 4)
    send(0, 0, 3, 0)
    loads[2].wait()

    def stage_group(g, c):
        lax.fori_loop(3 + g * TG, 3 + (g + 1) * TG, stage, 0)
        send(0, 3 + g * TG, TG, g + 1)
        return c

    lax.fori_loop(0, ngroups - 1, stage_group, 0)

    for s in range(SUBSTEPS):
        final = s == SUBSTEPS - 1

        def place_rows(f):
            S[s, f, pl.ds(7, lev, stride=stride), :] = rr[s, 0, f, 1]
            S[s, f, pl.ds(8 + rows, lev, stride=stride), :] = rr[s, 1, f, 0]
            S[s, f, pl.ds(9 + rows, lev, stride=stride), :] = rr[s, 1, f, 1]

        def side(f):
            return jnp.where(low8, cr[s, 0, f], cr[s, 1, f]), jnp.where(low8, cr[s, 0, f], cs[s, f])

        def core(f, l, d=0):
            return S[s, f, pl.ds(stride * l + 8 + d, rows), :]

        await_halo(s, 0, 3, 0)
        for f in range(3):
            place_rows(f)
        Ch, _ = side(0)
        Cu, Lu = side(1)
        aL = (COUR * 0.5 / 6.0) * (Lu + pltpu.roll(Lu, cols - 1, 1))
        bL = fcL * (rr[s, 0, 2, 1] + S[s, 2, pl.ds(8, lev, stride=stride), :])

        def prepare(i, carry):
            l = lev - 1 - i
            dx, dy = carry
            h, u, v = core(0, l), core(1, l), core(2, l)
            H = unpack(Ch, l)
            hp = pltpu.roll(jnp.where(first_lane, H, h), cols - 1, 1)
            hm = pltpu.roll(jnp.where(last_lane, H, h), 1, 1)
            up = pltpu.roll(jnp.where(first_lane, unpack(Cu, l), u), cols - 1, 1)
            As[l] = (COUR * 0.5 / 6.0) * (u + up)
            Bs[l] = facec[...] * (v + core(2, l, 1))
            dx = dx + (hp - hm)
            dy = dy + (core(0, l, 1) - core(0, l, -1))
            frc[1, l] = corr[...] * v - (COUR * 0.5 * GRAV) * dx
            frc[2, l] = -corr[...] * u - (COUR * 0.5 * GRAV) * dy
            return dx, dy

        zero = jnp.zeros((rows, cols), jnp.float32)
        lax.fori_loop(0, lev, prepare, (zero, zero), unroll=True)

        def field(f, c):
            @pl.when((f >= 3) & (lax.rem(f - 3, TG) == 0))
            def _():
                await_halo(s, f, TG, (f - 3) // TG + 1)

            place_rows(f)
            C, L = side(f)
            Lp = pltpu.roll(L, cols - 1, 1)
            FL = face(aL, pltpu.roll(L, 1, 1), L, Lp, pltpu.roll(L, cols - 2, 1))
            x0 = S[s, f, pl.ds(8, lev, stride=stride), :]
            x1 = S[s, f, pl.ds(9, lev, stride=stride), :]
            Gs[pl.ds(7, lev, stride=stride), :] = face(bL, rr[s, 0, f, 0], rr[s, 0, f, 1], x0, x1)
            kind = wind(f)

            def level(l, acc):
                x = core(f, l)
                H = unpack(C, l)
                xp = pltpu.roll(jnp.where(first_lane, H, x), cols - 1, 1)
                xpp = pltpu.roll(jnp.where(two_lanes, H, x), cols - 2, 1)
                xm = pltpu.roll(jnp.where(last_lane, H, x), 1, 1)
                F = face(As[l], xm, x, xp, xpp)
                Fl = pltpu.roll(jnp.where(last_lane, unpack(FL, l), F), 1, 1)
                G = face(Bs[l], core(f, l, -1), x, core(f, l, 1), core(f, l, 2))
                Gs[pl.ds(stride * l + 8, rows), :] = G
                Gl = Gs[pl.ds(stride * l + 7, rows), :]
                new = x - (F - Fl) - (G - Gl) * invc[...] + frc[kind, l]
                if final:
                    out[f, l] = new
                    return acc
                S[s + 1, f, pl.ds(stride * l + 8, rows), :] = new
                return pack(acc, new, l)

            acc0 = 0 if final else jnp.zeros((8, cols), jnp.float32)
            acc = lax.fori_loop(0, lev, level, acc0, unroll=True)
            if not final:
                cs[s + 1, f] = acc
                pack_rows(s + 1, f)

            @pl.when(f == 2)
            def _():
                if final:
                    pltpu.make_async_copy(out.at[0], ho, out_sem.at[0]).start()
                    pltpu.make_async_copy(out.at[pl.ds(1, 2)], wo, out_sem.at[1]).start()
                else:
                    send(s + 1, 0, 3, 0)

            @pl.when((f >= 3) & (lax.rem(f - 3, TG) == TG - 1))
            def _():
                f0 = f - TG + 1
                g = (f0 - 3) // TG + 1
                if final:
                    pltpu.make_async_copy(
                        out.at[pl.ds(f0, TG)], to.at[pl.ds(f0 - 3, TG)], out_sem.at[g + 1]
                    ).start()
                else:
                    send(s + 1, f0, TG, g)

            return c

        lax.fori_loop(0, nf, field, 0)

    for s in range(SUBSTEPS):
        for c in copies(s, 0, 3, 0):
            c.wait_send()

        def drain(g, c):
            for d in copies(s, 3 + g * TG, TG, g + 1):
                d.wait_send()
            return c

        lax.fori_loop(0, ngroups - 1, drain, 0)
    pltpu.make_async_copy(out.at[0], ho, out_sem.at[0]).wait()
    pltpu.make_async_copy(out.at[pl.ds(1, 2)], wo, out_sem.at[1]).wait()

    def flush(g, c):
        pltpu.make_async_copy(
            out.at[pl.ds(3 + g * TG, TG)], to.at[pl.ds(g * TG, TG)], out_sem.at[g + 2]
        ).wait()
        return c

    lax.fori_loop(0, ngroups - 1, flush, 0)


def shards(nlat, nlon, thickness, winds, tracer_mass):
    lev, rows, cols = thickness.shape
    ntr = tracer_mass.shape[0]
    nf = 3 + ntr
    groups = 1 + ntr // TG
    f32 = jnp.float32
    flat = lev * (rows + 8) + 8
    vm = pltpu.VMEM
    return pl.pallas_call(
        functools.partial(kernel, nlat, nlon),
        out_shape=[jax.ShapeDtypeStruct(a.shape, f32) for a in (thickness, winds, tracer_mass)],
        in_specs=[pl.BlockSpec(memory_space=pl.ANY)] * 3,
        out_specs=[pl.BlockSpec(memory_space=pl.ANY)] * 3,
        scratch_shapes=[
            vm((nf, lev, rows, cols), f32),
            vm((SUBSTEPS, nf, flat, cols), f32),
            vm((flat, cols), f32),
            vm((lev, rows, cols), f32),
            vm((lev, rows, cols), f32),
            vm((3, lev, rows, cols), f32),
            vm((rows, cols), f32),
            vm((rows, cols), f32),
            vm((rows, cols), f32),
            vm((SUBSTEPS, 2, nf, 2, lev, cols), f32),
            vm((SUBSTEPS, 2, nf, 2, lev, cols), f32),
            vm((SUBSTEPS, nf, 8, cols), f32),
            vm((SUBSTEPS, 2, nf, 8, cols), f32),
            vm((nf, lev, rows, cols), f32),
            pltpu.SemaphoreType.DMA((3,)),
            pltpu.SemaphoreType.DMA((groups + 1,)),
            pltpu.SemaphoreType.DMA((SUBSTEPS, 4, groups)),
            pltpu.SemaphoreType.DMA((SUBSTEPS, 4, groups)),
        ],
        compiler_params=pltpu.CompilerParams(
            collective_id=0, has_side_effects=True, vmem_limit_bytes=60 * 1024 * 1024
        ),
        cost_estimate=pl.CostEstimate(flops=30_000_000, bytes_accessed=3_000_000, transcendentals=0),
    )(thickness, winds, tracer_mass)


def solution(mesh):
    specs = (P(None, "lat", "lon"), P(None, None, "lat", "lon"), P(None, None, "lat", "lon"))
    return jax.shard_map(
        functools.partial(shards, mesh.shape["lat"], mesh.shape["lon"]),
        mesh=mesh,
        in_specs=specs,
        out_specs=specs,
        check_vma=False,
    )
```

time: 37.8 us -> 28.1 us (0.74)
  Pallas kernels: 31.5 us -> 22.7 us
  local copies, waits for them, and re-layouts: 5.4 us -> 4.58 us
    pallas_call x1, Pallas kernels: 31.5 us -> 22.7 us  [shards(): pl.pallas_call(functools.partial(kernel, nlat, nlon), out_shape=[jax.Shap...]
    unnamed x9 -> x5, local copies, waits for them, and re-layouts: 5.4 us -> 4.58 us
where the time goes in v2:
time: 28.1 us; the launch traced here: 27.9 us
  Pallas kernels  22.7 us (81%)
  local copies, waits for them, and re-layouts  4.58 us (16%)
  between operations  0.65 us (2%)
    pallas_call x1, Pallas kernels, shards(): pl.pallas_call(functools.partial(kernel, nlat, nlon), out_shape=[jax.Shap...  22.7 us
    unnamed x5, local copies, waits for them, and re-layouts  4.58 us

profile of v2, /device:TPU:0, one launch (start us, length us, event | category | flops | bytes accessed | tf_op | source)
XLA Modules:
  0.0 27.9 jit_solution(16546052408598195830)
XLA Ops:
  0.6 22.7 %shard_map.58 = (f32[8,32,128]{2,1,0:T(8,128)}, f32[2,8,32,128]{3,2,1,0:T(8,128)}, f32[8,8,32,128]{3,2,1,0:T(8,128)}) custom-call(f32[8,32,128]{2,1,0:T(8,128)} %h_hbm.1, f32[2,8,32,128]{3,2,1,0:T(8,128)} %w_hbm.1, f32[8,8,32,128]{3,2,1,0:T(8,128)} %t_hbm.1), custom_call_target="tpu_custom_call" | custom-call | flops 30000000 | bytes 3000000 | tf_op jit(solution)/shard_map/pallas_call | solution.py:280
  23.3 0.0 copy-start
  23.3 1.6 %copy.9 = f32[8,32,128]{2,1,0:T(8,128)} copy(f32[8,32,128]{2,1,0:T(8,128)} %get-tuple-element.6) | data formatting | bytes 262144
  24.9 0.0 copy-done
  24.9 0.7 %copy.10 = f32[2,8,32,128]{3,2,1,0:T(8,128)} copy(f32[2,8,32,128]{3,2,1,0:T(8,128)S(1)} %copy-done) | data formatting | bytes 524288
  25.6 2.3 %copy.11 = f32[8,8,32,128]{3,2,1,0:T(8,128)} copy(f32[8,8,32,128]{3,2,1,0:T(8,128)} %get-tuple-element.8) | data formatting | bytes 2097152
Async XLA Ops:
  23.3 1.6 %copy-start = (f32[2,8,32,128]{3,2,1,0:T(8,128)S(1)}, f32[2,8,32,128]{3,2,1,0:T(8,128)}, u32[]{:S(2)}) copy-start(f32[2,8,32,128]{3,2,1,0:T(8,128)} %get-tuple-element.7) | copy-start | bytes 786436

commit v3 on v2

--- a/solution.py
+++ b/solution.py
@@ -16,8 +16,8 @@
 MESH = pl.DeviceIdType.MESH
 
 
-def kernel(nlat, nlon, h_hbm, w_hbm, t_hbm, ho, wo, to, xin, S, Gs, As, Bs, frc, invc, corr, facec,
-           rs, rr, cs, cr, out, in_sem, out_sem, send_sem, recv_sem):
+def kernel(nlat, nlon, h_hbm, w_hbm, t_hbm, out, xin, S, Gs, As, Bs, frc, invc, corr, facec,
+           rs, rr, cs, cr, in_sem, send_sem, recv_sem):
     nf, lev, rows, cols = xin.shape
     ngroups = 1 + (nf - 3) // TG
     G8 = rows // 8
@@ -86,8 +86,8 @@
     def pack_rows(s, f):
         is_v = wind(f) // 2
         for r in range(2):
-            lo = S[s, f, pl.ds(8 + r + first * (1 - 2 * r), lev, stride=stride), :]
-            hi = S[s, f, pl.ds(8 + rows - 2 + r + last * (1 - 2 * r), lev, stride=stride), :]
+            lo = S[lax.rem(s, 2), f, pl.ds(8 + r + first * (1 - 2 * r), lev, stride=stride), :]
+            hi = S[lax.rem(s, 2), f, pl.ds(8 + rows - 2 + r + last * (1 - 2 * r), lev, stride=stride), :]
             rs[s, 0, f, r] = lo * (1 - 2 * first * is_v).astype(jnp.float32)
             rs[s, 1, f, r] = hi * (1 - 2 * last * is_v).astype(jnp.float32)
 
@@ -145,19 +145,20 @@
 
     lax.fori_loop(0, ngroups - 1, stage_group, 0)
 
-    for s in range(SUBSTEPS):
-        final = s == SUBSTEPS - 1
+    def substep(s, carry):
+        more = s < SUBSTEPS - 1
+        spare = 1 - lax.rem(s, 2)
 
         def place_rows(f):
-            S[s, f, pl.ds(7, lev, stride=stride), :] = rr[s, 0, f, 1]
-            S[s, f, pl.ds(8 + rows, lev, stride=stride), :] = rr[s, 1, f, 0]
-            S[s, f, pl.ds(9 + rows, lev, stride=stride), :] = rr[s, 1, f, 1]
+            S[1 - spare, f, pl.ds(7, lev, stride=stride), :] = rr[s, 0, f, 1]
+            S[1 - spare, f, pl.ds(8 + rows, lev, stride=stride), :] = rr[s, 1, f, 0]
+            S[1 - spare, f, pl.ds(9 + rows, lev, stride=stride), :] = rr[s, 1, f, 1]
 
         def side(f):
             return jnp.where(low8, cr[s, 0, f], cr[s, 1, f]), jnp.where(low8, cr[s, 0, f], cs[s, f])
 
         def core(f, l, d=0):
-            return S[s, f, pl.ds(stride * l + 8 + d, rows), :]
+            return S[1 - spare, f, pl.ds(stride * l + 8 + d, rows), :]
 
         await_halo(s, 0, 3, 0)
         for f in range(3):
@@ -165,7 +166,7 @@
         Ch, _ = side(0)
         Cu, Lu = side(1)
         aL = (COUR * 0.5 / 6.0) * (Lu + pltpu.roll(Lu, cols - 1, 1))
-        bL = fcL * (rr[s, 0, 2, 1] + S[s, 2, pl.ds(8, lev, stride=stride), :])
+        bL = fcL * (rr[s, 0, 2, 1] + S[1 - spare, 2, pl.ds(8, lev, stride=stride), :])
 
         def prepare(i, carry):
             l = lev - 1 - i
@@ -195,8 +196,8 @@
             C, L = side(f)
             Lp = pltpu.roll(L, cols - 1, 1)
             FL = face(aL, pltpu.roll(L, 1, 1), L, Lp, pltpu.roll(L, cols - 2, 1))
-            x0 = S[s, f, pl.ds(8, lev, stride=stride), :]
-            x1 = S[s, f, pl.ds(9, lev, stride=stride), :]
+            x0 = S[1 - spare, f, pl.ds(8, lev, stride=stride), :]
+            x1 = S[1 - spare, f, pl.ds(9, lev, stride=stride), :]
             Gs[pl.ds(7, lev, stride=stride), :] = face(bL, rr[s, 0, f, 0], rr[s, 0, f, 1], x0, x1)
             kind = wind(f)
 
@@ -212,40 +213,31 @@
                 Gs[pl.ds(stride * l + 8, rows), :] = G
                 Gl = Gs[pl.ds(stride * l + 7, rows), :]
                 new = x - (F - Fl) - (G - Gl) * invc[...] + frc[kind, l]
-                if final:
-                    out[f, l] = new
-                    return acc
-                S[s + 1, f, pl.ds(stride * l + 8, rows), :] = new
+                out[f, l] = new
+                S[spare, f, pl.ds(stride * l + 8, rows), :] = new
                 return pack(acc, new, l)
 
-            acc0 = 0 if final else jnp.zeros((8, cols), jnp.float32)
-            acc = lax.fori_loop(0, lev, level, acc0, unroll=True)
-            if not final:
+            acc = lax.fori_loop(0, lev, level, jnp.zeros((8, cols), jnp.float32), unroll=True)
+
+            @pl.when(more)
+            def _():
                 cs[s + 1, f] = acc
                 pack_rows(s + 1, f)
 
-            @pl.when(f == 2)
+            @pl.when(more & (f == 2))
             def _():
-                if final:
-                    pltpu.make_async_copy(out.at[0], ho, out_sem.at[0]).start()
-                    pltpu.make_async_copy(out.at[pl.ds(1, 2)], wo, out_sem.at[1]).start()
-                else:
-                    send(s + 1, 0, 3, 0)
-
-            @pl.when((f >= 3) & (lax.rem(f - 3, TG) == TG - 1))
+                send(s + 1, 0, 3, 0)
+
+            @pl.when(more & (f >= 3) & (lax.rem(f - 3, TG) == TG - 1))
             def _():
-                f0 = f - TG + 1
-                g = (f0 - 3) // TG + 1
-                if final:
-                    pltpu.make_async_copy(
-                        out.at[pl.ds(f0, TG)], to.at[pl.ds(f0 - 3, TG)], out_sem.at[g + 1]
-                    ).start()
-                else:
-                    send(s + 1, f0, TG, g)
+                send(s + 1, f - TG + 1, TG, (f - 3) // TG + 1)
 
             return c
 
         lax.fori_loop(0, nf, field, 0)
+        return carry
+
+    lax.fori_loop(0, SUBSTEPS, substep, 0)
 
     for s in range(SUBSTEPS):
         for c in copies(s, 0, 3, 0):
@@ -257,16 +249,17 @@
             return c
 
         lax.fori_loop(0, ngroups - 1, drain, 0)
-    pltpu.make_async_copy(out.at[0], ho, out_sem.at[0]).wait()
-    pltpu.make_async_copy(out.at[pl.ds(1, 2)], wo, out_sem.at[1]).wait()
-
-    def flush(g, c):
-        pltpu.make_async_copy(
-            out.at[pl.ds(3 + g * TG, TG)], to.at[pl.ds(g * TG, TG)], out_sem.at[g + 2]
-        ).wait()
-        return c
-
-    lax.fori_loop(0, ngroups - 1, flush, 0)
+
+def store_kernel(state, ho, wo, to, sem):
+    moves = [
+        pltpu.make_async_copy(state.at[pl.ds(3, to.shape[0])], to, sem.at[0]),
+        pltpu.make_async_copy(state.at[pl.ds(1, 2)], wo, sem.at[1]),
+        pltpu.make_async_copy(state.at[0], ho, sem.at[2]),
+    ]
+    for move in moves:
+        move.start()
+    for move in moves:
+        move.wait()
 
 
 def shards(nlat, nlon, thickness, winds, tracer_mass):
@@ -277,11 +270,11 @@
     f32 = jnp.float32
     flat = lev * (rows + 8) + 8
     vm = pltpu.VMEM
-    return pl.pallas_call(
+    state = pl.pallas_call(
         functools.partial(kernel, nlat, nlon),
-        out_shape=[jax.ShapeDtypeStruct(a.shape, f32) for a in (thickness, winds, tracer_mass)],
-        in_specs=[pl.BlockSpec(memory_space=pl.ANY)] * 3,
-        out_specs=[pl.BlockSpec(memory_space=pl.ANY)] * 3,
+        out_shape=pltpu.VMEM((nf, lev, rows, cols), f32),
+        in_specs=[pl.BlockSpec(memory_space=pltpu.HBM)] * 3,
+        out_specs=pl.BlockSpec(memory_space=pltpu.VMEM),
         scratch_shapes=[
             vm((nf, lev, rows, cols), f32),
             vm((SUBSTEPS, nf, flat, cols), f32),
@@ -296,17 +289,23 @@
             vm((SUBSTEPS, 2, nf, 2, lev, cols), f32),
             vm((SUBSTEPS, nf, 8, cols), f32),
             vm((SUBSTEPS, 2, nf, 8, cols), f32),
-            vm((nf, lev, rows, cols), f32),
             pltpu.SemaphoreType.DMA((3,)),
-            pltpu.SemaphoreType.DMA((groups + 1,)),
             pltpu.SemaphoreType.DMA((SUBSTEPS, 4, groups)),
             pltpu.SemaphoreType.DMA((SUBSTEPS, 4, groups)),
         ],
         compiler_params=pltpu.CompilerParams(
-            collective_id=0, has_side_effects=True, vmem_limit_bytes=60 * 1024 * 1024
+            collective_id=0, has_side_effects=True, vmem_limit_bytes=56 * 1024 * 1024
         ),
         cost_estimate=pl.CostEstimate(flops=30_000_000, bytes_accessed=3_000_000, transcendentals=0),
     )(thickness, winds, tracer_mass)
+    return pl.pallas_call(
+        store_kernel,
+        out_shape=[jax.ShapeDtypeStruct(a.shape, f32) for a in (thickness, winds, tracer_mass)],
+        in_specs=[pl.BlockSpec(memory_space=pltpu.VMEM)],
+        out_specs=[pl.BlockSpec(memory_space=pltpu.HBM)] * 3,
+        scratch_shapes=[pltpu.SemaphoreType.DMA((3,))],
+        compiler_params=pltpu.CompilerParams(vmem_limit_bytes=8 * 1024 * 1024),
+    )(state)
 
 
 def solution(mesh):

time: 28.1 us -> 45.7 us (1.63)
  Pallas kernels: 22.7 us -> 44.9 us
  local copies, waits for them, and re-layouts: 4.58 us -> 0 us
    pallas_call x1 -> x2, Pallas kernels: 22.7 us -> 44.9 us  [the longest x1 43.8 us: shards(): pl.pallas_call(functools.partial(kernel, nlat, nlon), out_shape=pltpu.VME...]
    unnamed x5 -> x0, local copies, waits for them, and re-layouts: 4.58 us -> none
where the time goes in v3:
time: 45.7 us; the launch traced here: 45.5 us
  Pallas kernels  44.9 us (98%)
  between operations  0.64 us (1%)
    pallas_call x1, Pallas kernels, shards(): pl.pallas_call(functools.partial(kernel, nlat, nlon), out_shape=pltpu.VME...  43.8 us
    pallas_call x1, Pallas kernels, shards(): pl.pallas_call(store_kernel, out_shape=[jax.ShapeDtypeStruct(a.shape, f32...  1.11 us

profile of v3, /device:TPU:0, one launch (start us, length us, event | category | flops | bytes accessed | tf_op | source)
XLA Modules:
  0.0 45.5 jit_solution(15775788242750879696)
XLA Ops:
  0.6 43.8 %shard_map.58.state = f32[11,8,32,128]{3,2,1,0:T(8,128)S(1)} custom-call(f32[8,32,128]{2,1,0:T(8,128)} %h_hbm.1, f32[2,8,32,128]{3,2,1,0:T(8,128)} %w_hbm.1, f32[8,8,32,128]{3,2,1,0:T(8,128)} %t_hbm.1), custom_call_target="tpu_custom_call" | custom-call | flops 30000000 | bytes 3000000 | tf_op jit(solution)/shard_map/pallas_call | solution.py:273
  44.4 1.1 %shard_map.59 = (f32[8,32,128]{2,1,0:T(8,128)}, f32[2,8,32,128]{3,2,1,0:T(8,128)}, f32[8,8,32,128]{3,2,1,0:T(8,128)}) custom-call(f32[11,8,32,128]{3,2,1,0:T(8,128)S(1)} %shard_map.58.state), custom_call_target="tpu_custom_call" | custom-call | tf_op jit(solution)/shard_map/pallas_call | solution.py:301

commit v4 on v3

--- a/solution.py
+++ b/solution.py
@@ -16,9 +16,10 @@
 MESH = pl.DeviceIdType.MESH
 
 
-def kernel(nlat, nlon, h_hbm, w_hbm, t_hbm, out, xin, S, Gs, As, Bs, frc, invc, corr, facec,
+def kernel(nlat, nlon, h_hbm, w_hbm, t_hbm, out, xin, S0, S1, Gs, As, Bs, frc, invc, corr, facec,
            rs, rr, cs, cr, in_sem, send_sem, recv_sem):
     nf, lev, rows, cols = xin.shape
+    S = (S0, S1)
     ngroups = 1 + (nf - 3) // TG
     G8 = rows // 8
     stride = rows + 8
@@ -86,8 +87,8 @@
     def pack_rows(s, f):
         is_v = wind(f) // 2
         for r in range(2):
-            lo = S[lax.rem(s, 2), f, pl.ds(8 + r + first * (1 - 2 * r), lev, stride=stride), :]
-            hi = S[lax.rem(s, 2), f, pl.ds(8 + rows - 2 + r + last * (1 - 2 * r), lev, stride=stride), :]
+            lo = S[s][f, pl.ds(8 + r + first * (1 - 2 * r), lev, stride=stride), :]
+            hi = S[s][f, pl.ds(8 + rows - 2 + r + last * (1 - 2 * r), lev, stride=stride), :]
             rs[s, 0, f, r] = lo * (1 - 2 * first * is_v).astype(jnp.float32)
             rs[s, 1, f, r] = hi * (1 - 2 * last * is_v).astype(jnp.float32)
 
@@ -124,7 +125,7 @@
     def stage(f, c):
         def level(l, acc):
             x = xin[f, l]
-            S[0, f, pl.ds(stride * l + 8, rows), :] = x
+            S[0][f, pl.ds(stride * l + 8, rows), :] = x
             return pack(acc, x, l)
 
         cs[0, f] = lax.fori_loop(0, lev, level, jnp.zeros((8, cols), jnp.float32), unroll=True)
@@ -145,20 +146,19 @@
 
     lax.fori_loop(0, ngroups - 1, stage_group, 0)
 
-    def substep(s, carry):
-        more = s < SUBSTEPS - 1
-        spare = 1 - lax.rem(s, 2)
+    for s in range(SUBSTEPS):
+        final = s == SUBSTEPS - 1
 
         def place_rows(f):
-            S[1 - spare, f, pl.ds(7, lev, stride=stride), :] = rr[s, 0, f, 1]
-            S[1 - spare, f, pl.ds(8 + rows, lev, stride=stride), :] = rr[s, 1, f, 0]
-            S[1 - spare, f, pl.ds(9 + rows, lev, stride=stride), :] = rr[s, 1, f, 1]
+            S[s][f, pl.ds(7, lev, stride=stride), :] = rr[s, 0, f, 1]
+            S[s][f, pl.ds(8 + rows, lev, stride=stride), :] = rr[s, 1, f, 0]
+            S[s][f, pl.ds(9 + rows, lev, stride=stride), :] = rr[s, 1, f, 1]
 
         def side(f):
             return jnp.where(low8, cr[s, 0, f], cr[s, 1, f]), jnp.where(low8, cr[s, 0, f], cs[s, f])
 
         def core(f, l, d=0):
-            return S[1 - spare, f, pl.ds(stride * l + 8 + d, rows), :]
+            return S[s][f, pl.ds(stride * l + 8 + d, rows), :]
 
         await_halo(s, 0, 3, 0)
         for f in range(3):
@@ -166,7 +166,7 @@
         Ch, _ = side(0)
         Cu, Lu = side(1)
         aL = (COUR * 0.5 / 6.0) * (Lu + pltpu.roll(Lu, cols - 1, 1))
-        bL = fcL * (rr[s, 0, 2, 1] + S[1 - spare, 2, pl.ds(8, lev, stride=stride), :])
+        bL = fcL * (rr[s, 0, 2, 1] + S[s][2, pl.ds(8, lev, stride=stride), :])
 
         def prepare(i, carry):
             l = lev - 1 - i
@@ -196,8 +196,8 @@
             C, L = side(f)
             Lp = pltpu.roll(L, cols - 1, 1)
             FL = face(aL, pltpu.roll(L, 1, 1), L, Lp, pltpu.roll(L, cols - 2, 1))
-            x0 = S[1 - spare, f, pl.ds(8, lev, stride=stride), :]
-            x1 = S[1 - spare, f, pl.ds(9, lev, stride=stride), :]
+            x0 = S[s][f, pl.ds(8, lev, stride=stride), :]
+            x1 = S[s][f, pl.ds(9, lev, stride=stride), :]
             Gs[pl.ds(7, lev, stride=stride), :] = face(bL, rr[s, 0, f, 0], rr[s, 0, f, 1], x0, x1)
             kind = wind(f)
 
@@ -213,31 +213,32 @@
                 Gs[pl.ds(stride * l + 8, rows), :] = G
                 Gl = Gs[pl.ds(stride * l + 7, rows), :]
                 new = x - (F - Fl) - (G - Gl) * invc[...] + frc[kind, l]
-                out[f, l] = new
-                S[spare, f, pl.ds(stride * l + 8, rows), :] = new
+                if final:
+                    out[f, l] = new
+                    return acc
+                S[s + 1][f, pl.ds(stride * l + 8, rows), :] = new
                 return pack(acc, new, l)
 
-            acc = lax.fori_loop(0, lev, level, jnp.zeros((8, cols), jnp.float32), unroll=True)
-
-            @pl.when(more)
-            def _():
+            acc0 = 0 if final else jnp.zeros((8, cols), jnp.float32)
+            acc = lax.fori_loop(0, lev, level, acc0, unroll=True)
+            if not final:
                 cs[s + 1, f] = acc
                 pack_rows(s + 1, f)
 
-            @pl.when(more & (f == 2))
+            if final:
+                return c
+
+            @pl.when(f == 2)
             def _():
                 send(s + 1, 0, 3, 0)
 
-            @pl.when(more & (f >= 3) & (lax.rem(f - 3, TG) == TG - 1))
+            @pl.when((f >= 3) & (lax.rem(f - 3, TG) == TG - 1))
             def _():
                 send(s + 1, f - TG + 1, TG, (f - 3) // TG + 1)
 
             return c
 
         lax.fori_loop(0, nf, field, 0)
-        return carry
-
-    lax.fori_loop(0, SUBSTEPS, substep, 0)
 
     for s in range(SUBSTEPS):
         for c in copies(s, 0, 3, 0):
@@ -277,7 +278,8 @@
         out_specs=pl.BlockSpec(memory_space=pltpu.VMEM),
         scratch_shapes=[
             vm((nf, lev, rows, cols), f32),
-            vm((SUBSTEPS, nf, flat, cols), f32),
+            vm((nf, flat, cols), f32),
+            vm((nf, flat, cols), f32),
             vm((flat, cols), f32),
             vm((lev, rows, cols), f32),
             vm((lev, rows, cols), f32),

time: 45.7 us -> 23.9 us (0.52)
  Pallas kernels: 44.9 us -> 23.1 us
    pallas_call x1, Pallas kernels: 43.8 us -> 22 us  [shards(): pl.pallas_call(functools.partial(kernel, nlat, nlon), out_shape=pltpu.VME...]
where the time goes in v4:
time: 23.9 us; the launch traced here: 23.7 us
  Pallas kernels  23.1 us (97%)
  between operations  0.64 us (3%)
    pallas_call x1, Pallas kernels, shards(): pl.pallas_call(functools.partial(kernel, nlat, nlon), out_shape=pltpu.VME...  22 us
    pallas_call x1, Pallas kernels, shards(): pl.pallas_call(store_kernel, out_shape=[jax.ShapeDtypeStruct(a.shape, f32...  1.11 us

profile of v4, /device:TPU:0, one launch (start us, length us, event | category | flops | bytes accessed | tf_op | source)
XLA Modules:
  0.0 23.7 jit_solution(16084834434142554928)
XLA Ops:
  0.6 22.0 %shard_map.58.state = f32[11,8,32,128]{3,2,1,0:T(8,128)S(1)} custom-call(f32[8,32,128]{2,1,0:T(8,128)} %h_hbm.1, f32[2,8,32,128]{3,2,1,0:T(8,128)} %w_hbm.1, f32[8,8,32,128]{3,2,1,0:T(8,128)} %t_hbm.1), custom_call_target="tpu_custom_call" | custom-call | flops 30000000 | bytes 3000000 | tf_op jit(solution)/shard_map/pallas_call | solution.py:274
  22.6 1.1 %shard_map.59 = (f32[8,32,128]{2,1,0:T(8,128)}, f32[2,8,32,128]{3,2,1,0:T(8,128)}, f32[8,8,32,128]{3,2,1,0:T(8,128)}) custom-call(f32[11,8,32,128]{3,2,1,0:T(8,128)S(1)} %shard_map.58.state), custom_call_target="tpu_custom_call" | custom-call | tf_op jit(solution)/shard_map/pallas_call | solution.py:303

commit v5 on v4

--- a/solution.py
+++ b/solution.py
@@ -66,9 +66,10 @@
     last_lane = lane >= cols - 1
 
     def face(speed, behind, centre, forward, beyond):
-        return speed * jnp.where(
-            speed >= 0.0, 5.0 * centre + 2.0 * forward - behind, 5.0 * forward + 2.0 * centre - beyond
-        )
+        along = speed >= 0.0
+        near = jnp.where(along, centre, forward)
+        far = jnp.where(along, behind, beyond)
+        return speed * (2.0 * (centre + forward) + (3.0 * near - far))
 
     def pack(acc, x, l):
         for rg in range(G8):

time: 23.9 us -> 23.9 us (level)
  no operation moved by 1% of the time
where the time goes in v5:
time: 23.9 us; the launch traced here: 23.8 us
  Pallas kernels  23.1 us (97%)
  between operations  0.64 us (3%)
    pallas_call x1, Pallas kernels, shards(): pl.pallas_call(functools.partial(kernel, nlat, nlon), out_shape=pltpu.VME...  22 us
    pallas_call x1, Pallas kernels, shards(): pl.pallas_call(store_kernel, out_shape=[jax.ShapeDtypeStruct(a.shape, f32...  1.11 us

profile of v5, /device:TPU:0, one launch (start us, length us, event | category | flops | bytes accessed | tf_op | source)
XLA Modules:
  0.0 23.8 jit_solution(13134631873840969888)
XLA Ops:
  0.6 22.0 %shard_map.58.state = f32[11,8,32,128]{3,2,1,0:T(8,128)S(1)} custom-call(f32[8,32,128]{2,1,0:T(8,128)} %h_hbm.1, f32[2,8,32,128]{3,2,1,0:T(8,128)} %w_hbm.1, f32[8,8,32,128]{3,2,1,0:T(8,128)} %t_hbm.1), custom_call_target="tpu_custom_call" | custom-call | flops 30000000 | bytes 3000000 | tf_op jit(solution)/shard_map/pallas_call | solution.py:275
  22.7 1.1 %shard_map.59 = (f32[8,32,128]{2,1,0:T(8,128)}, f32[2,8,32,128]{3,2,1,0:T(8,128)}, f32[8,8,32,128]{3,2,1,0:T(8,128)}) custom-call(f32[11,8,32,128]{3,2,1,0:T(8,128)S(1)} %shard_map.58.state), custom_call_target="tpu_custom_call" | custom-call | tf_op jit(solution)/shard_map/pallas_call | solution.py:304

commit v6 on v5

--- a/solution.py
+++ b/solution.py
@@ -12,7 +12,7 @@
 COUR = 0.25
 GRAV = 1.0
 FCOR = 1.0
-TG = 2
+TG = 1
 MESH = pl.DeviceIdType.MESH
 
 

time: 23.9 us -> 24.3 us (1.017)
  Pallas kernels: 23.1 us -> 23.5 us
    pallas_call x1, Pallas kernels: 22 us -> 22.4 us  [shards(): pl.pallas_call(functools.partial(kernel, nlat, nlon), out_shape=pltpu.VME...]
where the time goes in v6:
time: 24.3 us; the launch traced here: 24.1 us
  Pallas kernels  23.5 us (97%)
  between operations  0.64 us (3%)
    pallas_call x1, Pallas kernels, shards(): pl.pallas_call(functools.partial(kernel, nlat, nlon), out_shape=pltpu.VME...  22.4 us
    pallas_call x1, Pallas kernels, shards(): pl.pallas_call(store_kernel, out_shape=[jax.ShapeDtypeStruct(a.shape, f32...  1.11 us

profile of v6, /device:TPU:0, one launch (start us, length us, event | category | flops | bytes accessed | tf_op | source)
XLA Modules:
  0.0 24.1 jit_solution(5054122974551073545)
XLA Ops:
  0.6 22.4 %shard_map.58.state = f32[11,8,32,128]{3,2,1,0:T(8,128)S(1)} custom-call(f32[8,32,128]{2,1,0:T(8,128)} %h_hbm.1, f32[2,8,32,128]{3,2,1,0:T(8,128)} %w_hbm.1, f32[8,8,32,128]{3,2,1,0:T(8,128)} %t_hbm.1), custom_call_target="tpu_custom_call" | custom-call | flops 30000000 | bytes 3000000 | tf_op jit(solution)/shard_map/pallas_call | solution.py:275
  23.0 1.1 %shard_map.59 = (f32[8,32,128]{2,1,0:T(8,128)}, f32[2,8,32,128]{3,2,1,0:T(8,128)}, f32[8,8,32,128]{3,2,1,0:T(8,128)}) custom-call(f32[11,8,32,128]{3,2,1,0:T(8,128)S(1)} %shard_map.58.state), custom_call_target="tpu_custom_call" | custom-call | tf_op jit(solution)/shard_map/pallas_call | solution.py:304
